TPU v7x, 128 devices: a whole 4x4x4 slice. The times are simulated.
128 devices in a mesh: scan: 16 (over z, x), tile: 8 (over y, core).
Axes of the slice: x: 4, y: 4, z: 4, core: 2. Of those that a mesh axis runs over, the one named last changes fastest.
Arguments:
- object_planes: float32 [2, 8192, 8192], P(None, 'scan', 'tile'), may hold values from -5 to 5
- probe_planes: float32 [2, 512, 512], replicated, may hold values from -5 to 5
- amplitudes: float32 [768, 512, 512], P(('scan', 'tile')), may hold values from 0.3 to 2
- off_rows: int32 [768], P(('scan', 'tile')), may hold values from 0 to 511
- off_cols: int32 [768], P(('scan', 'tile')), may hold values from 0 to 1023
Outputs:
- object_grad: float32 [2, 8192, 8192], P(None, 'scan', 'tile')
- probe_grad: float32 [2, 512, 512], replicated
Inputs may be any that keep to these rules, and one draw needn't show every extreme that they name: off_rows[k] is the row offset of position k inside the tile of its device, the device k // 6 in the order scan then tile. off_cols[k] is the column offset of position k inside the tile of its device.
All inputs are finite; a program needn't handle non-finite values.
Results may differ from a plain program's by a relative error of at most 0.0054.
The roundings to bfloat16 on the way count: a program that leaves them out, or rounds other values in their place, can miss the bound.
Values sent between devices are 32-bit elements; how exact they have to be, the bound alone decides.
No kernel may reach another device: no remote copies, remote signals or barrier semaphores. Data moves between devices by JAX's collectives and lax.ppermute only.
A program may use at most 128 MiB of HBM per device.

v0:
```python
import jax
import jax.numpy as jnp
from jax import lax
from jax.sharding import PartitionSpec as P


def shifted(value, axis, steps):
    count = lax.axis_size(axis)
    pairs = [(source, (source + steps) % count) for source in range(count)]
    return lax.ppermute(value, axis, pairs)


def dft_tables(width):
    counter = jnp.arange(width, dtype=jnp.int32)
    product = counter[:, None] * counter[None, :] % width
    angles = product.astype(jnp.float32) * (2.0 * 3.141592653589793 / width)
    norm_scale = 1.0 / jnp.sqrt(jnp.float32(width))
    return (
        (jnp.cos(angles) * norm_scale).astype(jnp.bfloat16),
        (jnp.sin(angles) * norm_scale).astype(jnp.bfloat16),
    )


def left_product(table, planes):
    return jnp.einsum("cdua,dab->cub", table, planes, preferred_element_type=jnp.float32)


def right_product(planes, table):
    return jnp.einsum("dub,dcbv->cuv", planes, table, preferred_element_type=jnp.float32)


def body(object_planes, probe_planes, amplitudes, off_rows, off_cols):
    width = probe_planes.shape[1]
    rows_here = object_planes.shape[1]
    cols_here = object_planes.shape[2]
    count = amplitudes.shape[0]
    cosine, sine = dft_tables(width)
    table_plus = jnp.stack([jnp.stack([cosine, sine]), jnp.stack([-sine, cosine])])
    table_minus = jnp.stack([jnp.stack([cosine, -sine]), jnp.stack([sine, cosine])])
    probe_real = probe_planes[0]
    probe_imag = probe_planes[1]
    below_rows = shifted(object_planes, "scan", -1)
    taller = jnp.concatenate([object_planes, below_rows], axis=1)
    beside = shifted(taller[:, :, :width], "tile", -1)
    extended = jnp.concatenate([taller, beside], axis=2)

    def visit(position, carried):
        gradient, probe_sum = carried
        row_start = off_rows[position]
        col_start = off_cols[position]
        anchor = jnp.zeros((), jnp.int32)
        patch = lax.dynamic_slice(extended, (anchor, row_start, col_start), (2, width, width))
        psi = jnp.stack(
            [
                probe_real * patch[0] - probe_imag * patch[1],
                probe_real * patch[1] + probe_imag * patch[0],
            ]
        ).astype(jnp.bfloat16)
        half = left_product(table_plus, psi).astype(jnp.bfloat16)
        far = right_product(half, table_minus)
        magnitude = jnp.sqrt(far[0] * far[0] + far[1] * far[1])
        factor = 1.0 - amplitudes[position] / jnp.maximum(magnitude, 0.5)
        misfit = (far * factor[None]).astype(jnp.bfloat16)
        back = left_product(table_minus, misfit).astype(jnp.bfloat16)
        wave = right_product(back, table_plus)
        update = jnp.stack(
            [
                probe_real * wave[0] + probe_imag * wave[1],
                probe_real * wave[1] - probe_imag * wave[0],
            ]
        )
        current = lax.dynamic_slice(gradient, (anchor, row_start, col_start), (2, width, width))
        gradient = lax.dynamic_update_slice(
            gradient, current + update, (anchor, row_start, col_start)
        )
        probe_sum = probe_sum + jnp.stack(
            [patch[0] * wave[0] + patch[1] * wave[1], patch[0] * wave[1] - patch[1] * wave[0]]
        )
        return (gradient, probe_sum)

    start = (jnp.zeros(extended.shape, jnp.float32), jnp.zeros((2, width, width), jnp.float32))
    gradient, probe_sum = lax.fori_loop(0, count, visit, start)
    right_strip = shifted(gradient[:, :, cols_here:], "tile", 1)
    gradient = gradient[:, :, :cols_here].at[:, :, :width].add(right_strip)
    lower_rows = shifted(gradient[:, rows_here:, :], "scan", 1)
    gradient = gradient[:, :rows_here, :].at[:, :width, :].add(lower_rows)
    summed = lax.psum(probe_sum, ("scan", "tile"))
    npos_total = count * lax.axis_size("scan") * lax.axis_size("tile")
    return (gradient, summed / jnp.sqrt(jnp.float32(npos_total)))


def solution(mesh):
    in_specs = (
        P(None, "scan", "tile"),
        P(),
        P(("scan", "tile"), None, None),
        P(("scan", "tile")),
        P(("scan", "tile")),
    )
    out_specs = (P(None, "scan", "tile"), P())
    return jax.shard_map(body, mesh=mesh, in_specs=in_specs, out_specs=out_specs, check_vma=False)
```

profile of v0, /device:TPU:1, one launch (start us, length us, event | category | flops | bytes accessed | tf_op | source)
XLA Modules:
  0.0 729.7 jit_solution(16970426486811285647)
XLA Ops:
  7.2 6.8 collective-permute-start
  16.6 87.0 %collective-permute-done = f32[2,512,1024]{2,1,0:T(8,128)S(1)} collective-permute-done((f32[2,512,1024]{2,1,0:T(8,128)}, f32[2,512,1024]{2,1,0:T(8,128)S(1)}, u32[]{:S(2)}, u32[]{:S(2)}) %collective-permute-start) | collective-permute-done | bytes 4194336 | tf_op jit(solution)/shard_map/ppermute | solution.py:10
  110.3 4.0 fusion.37
  114.3 4.4 multiply_convert_fusion.1
  123.5 34.5 %collective-permute-done.1 = f32[2,1024,512]{2,1,0:T(8,128)} collective-permute-done((f32[2,1024,512]{2,1,0:T(8,128)}, f32[2,1024,512]{2,1,0:T(8,128)}, u32[]{:S(2)}, u32[]{:S(2)}) %collective-permute-start.1) | collective-permute-done | bytes 4194336 | tf_op jit(solution)/shard_map/ppermute | solution.py:10
  158.0 6.4 pad_maximum_fusion
  164.4 6.1 broadcast_in_dim.11
  170.5 269.9 %while.19 = (s32[]{:T(128)}, f32[2,1024,1536]{2,1,0:T(8,128)}, f32[2,512,512]{2,1,0:T(8,128)}, s32[6]{0:T(128)S(1)}, s32[6]{0:T(128)S(1)}, /*index=5*/f32[512,51...) while((s32[]{:T(128)}, f32[2,1024,1536]{2,1,0:T(8,128)}, ...), condition=%wide.region_1.2_spmd.clone, body=%wide.region_0.1_spmd.clone.sunk | while | flops 4308598784 | bytes 70254960 | solution.py:82
  175.5 3.8 fusion.56
  179.3 4.9 convolution_bitcast_fusion.4
  186.9 6.2 convolution_bitcast_fusion.5
  201.1 14.4 %dynamic_update_slice.9 = f32[2,1024,1536]{2,1,0:T(8,128)} dynamic-update-slice(f32[2,1024,1536]{2,1,0:T(8,128)} %get-tuple-element.410, f32[2,512,512]{2,1,0:T(8,128)S(1)} %get-tuple-element.391, s32[]{:T(128)} %constant.126.clone.1..sunk, s32[]{:T(128)S(6)} %select_n.77, s32[]{:T(128)S(6)} %select_n.78) | dynamic-update-slice | bytes 4194308 | tf_op jit(solution)/shard_map/while/body/eval_jaxpr/dynamic_update_slice | solution.py:73
  220.6 3.8 fusion.56
  224.4 4.9 convolution_bitcast_fusion.4
  232.0 6.2 convolution_bitcast_fusion.5
  246.2 14.3 %dynamic_update_slice.9 = f32[2,1024,1536]{2,1,0:T(8,128)} dynamic-update-slice(f32[2,1024,1536]{2,1,0:T(8,128)} %get-tuple-element.410, f32[2,512,512]{2,1,0:T(8,128)S(1)} %get-tuple-element.391, s32[]{:T(128)} %constant.126.clone.1..sunk, s32[]{:T(128)S(6)} %select_n.77, s32[]{:T(128)S(6)} %select_n.78) | dynamic-update-slice | bytes 4194308 | tf_op jit(solution)/shard_map/while/body/eval_jaxpr/dynamic_update_slice | solution.py:73
  269.3 4.9 convolution_bitcast_fusion.4
  276.9 6.2 convolution_bitcast_fusion.5
  291.1 14.4 %dynamic_update_slice.9 = f32[2,1024,1536]{2,1,0:T(8,128)} dynamic-update-slice(f32[2,1024,1536]{2,1,0:T(8,128)} %get-tuple-element.410, f32[2,512,512]{2,1,0:T(8,128)S(1)} %get-tuple-element.391, s32[]{:T(128)} %constant.126.clone.1..sunk, s32[]{:T(128)S(6)} %select_n.77, s32[]{:T(128)S(6)} %select_n.78) | dynamic-update-slice | bytes 4194308 | tf_op jit(solution)/shard_map/while/body/eval_jaxpr/dynamic_update_slice | solution.py:73
  314.4 4.9 convolution_bitcast_fusion.4
  321.9 6.2 convolution_bitcast_fusion.5
  336.2 14.4 %dynamic_update_slice.9 = f32[2,1024,1536]{2,1,0:T(8,128)} dynamic-update-slice(f32[2,1024,1536]{2,1,0:T(8,128)} %get-tuple-element.410, f32[2,512,512]{2,1,0:T(8,128)S(1)} %get-tuple-element.391, s32[]{:T(128)} %constant.126.clone.1..sunk, s32[]{:T(128)S(6)} %select_n.77, s32[]{:T(128)S(6)} %select_n.78) | dynamic-update-slice | bytes 4194308 | tf_op jit(solution)/shard_map/while/body/eval_jaxpr/dynamic_update_slice | solution.py:73
  359.4 4.9 convolution_bitcast_fusion.4
  367.0 6.2 convolution_bitcast_fusion.5
  381.3 14.1 %dynamic_update_slice.9 = f32[2,1024,1536]{2,1,0:T(8,128)} dynamic-update-slice(f32[2,1024,1536]{2,1,0:T(8,128)} %get-tuple-element.410, f32[2,512,512]{2,1,0:T(8,128)S(1)} %get-tuple-element.391, s32[]{:T(128)} %constant.126.clone.1..sunk, s32[]{:T(128)S(6)} %select_n.77, s32[]{:T(128)S(6)} %select_n.78) | dynamic-update-slice | bytes 4194308 | tf_op jit(solution)/shard_map/while/body/eval_jaxpr/dynamic_update_slice | solution.py:73
  404.2 4.9 convolution_bitcast_fusion.4
  411.8 6.2 convolution_bitcast_fusion.5
  426.0 14.4 %dynamic_update_slice.9 = f32[2,1024,1536]{2,1,0:T(8,128)} dynamic-update-slice(f32[2,1024,1536]{2,1,0:T(8,128)} %get-tuple-element.410, f32[2,512,512]{2,1,0:T(8,128)S(1)} %get-tuple-element.391, s32[]{:T(128)} %constant.126.clone.1..sunk, s32[]{:T(128)S(6)} %select_n.77, s32[]{:T(128)S(6)} %select_n.78) | dynamic-update-slice | bytes 4194308 | tf_op jit(solution)/shard_map/while/body/eval_jaxpr/dynamic_update_slice | solution.py:73
  443.1 4.2 slice.124
  447.3 41.2 %collective-permute-done.2 = f32[2,1024,512]{2,1,0:T(8,128)S(1)} collective-permute-done((f32[2,1024,512]{2,1,0:T(8,128)S(1)}, f32[2,1024,512]{2,1,0:T(8,128)S(1)}, u32[]{:S(2)}, u32[]{:S(2)}) %collective-permute-start.2) | collective-permute-done | bytes 4194336 | tf_op jit(solution)/shard_map/ppermute | solution.py:10
  496.3 216.5 %all-reduce.2.cloned.1.call-done = f32[2,512,512]{2,1,0:T(8,128)} async-done(((f32[2,512,512]{2,1,0:T(8,128)}), f32[2,512,512]{2,1,0:T(8,128)}) %all-reduce.2.cloned.1.call-update) | async-done | bytes 2097168 | tf_op jit(solution)/shard_map/psum | solution.py:87
  716.0 6.8 slice_add_fusion
  (92 shorter events, 113.9 us)
Async XLA Ops:
  7.2 705.7 %all-reduce.2.cloned.1.call-start = ((), (), s32[]{:S(2)}) async-start(), calls=%async_computation | async-start | bytes 4194304 | tf_op jit(solution)/shard_map/psum | solution.py:87
  7.2 96.4 %collective-permute-start = (f32[2,512,1024]{2,1,0:T(8,128)}, f32[2,512,1024]{2,1,0:T(8,128)S(1)}, u32[]{:S(2)}, u32[]{:S(2)}) collective-permute-start(f32[2,512,1024]{2,1,0:T(8,128)} %param.13), channel_id=1, source_target_pairs={{0,120},{8,0},{16,8},{24,16},{32,24},{40,32},{48,40},{56,48},{64,5... | collective-permute-start | bytes 12582920 | tf_op jit(solution)/shard_map/ppermute | solution.py:10
  104.2 4.6 copy-start.2
  108.8 49.2 %collective-permute-start.1 = (f32[2,1024,512]{2,1,0:T(8,128)}, f32[2,1024,512]{2,1,0:T(8,128)}, u32[]{:S(2)}, u32[]{:S(2)}) collective-permute-start(f32[2,1024,512]{2,1,0:T(8,128)} %slice.139), channel_id=1, source_target_pairs={{0,7},{1,0},{2,1},{3,2},{4,3},{5,4},{6,5},{7,6},{8,15},{9,8},{10,9... | collective-permute-start | bytes 12582920 | tf_op jit(solution)/shard_map/ppermute | solution.py:10
  119.0 39.0 %slice-start = ((s8[8388608]{0:T(1024)(128)(4,1)}), s8[4194304]{0:T(1024)(128)(4,1)S(1)}, s32[]{:S(2)}) async-start(s8[8388608]{0:T(1024)(128)(4,1)} %bitcast.140), calls=%async_computation.1 | async-start | bytes 8388608
  119.2 3.1 copy-start.4
  120.8 37.2 %slice-start.1 = ((s8[8388608]{0:T(1024)(128)(4,1)}), s8[4194304]{0:T(1024)(128)(4,1)S(1)}, s32[]{:S(2)}) async-start(s8[8388608]{0:T(1024)(128)(4,1)} %bitcast.140), calls=%async_computation.2 | async-start | bytes 8388608
  164.4 6.1 copy-start.5
  164.4 6.1 copy-start.6
  193.1 3.6 copy-start
  199.8 1.3 copy-start.1
  238.2 3.6 copy-start
  244.9 1.3 copy-start.1
  283.1 3.6 copy-start
  289.8 1.3 copy-start.1
  328.1 3.6 copy-start
  334.9 1.3 copy-start.1
  373.2 3.6 copy-start
  379.9 1.3 copy-start.1
  418.0 3.6 copy-start
  424.7 1.3 copy-start.1
  443.0 45.5 %collective-permute-start.2 = (f32[2,1024,512]{2,1,0:T(8,128)S(1)}, f32[2,1024,512]{2,1,0:T(8,128)S(1)}, u32[]{:S(2)}, u32[]{:S(2)}) collective-permute-start(f32[2,1024,512]{2,1,0:T(8,128)S(1)} %slice.126), channel_id=1, source_target_pairs={{0,1},{1,2},{2,3},{3,4},{4,5},{5,6},{6,7},{7,0},{8,9},{9,10},{10,1... | collective-permute-start | bytes 12582920 | tf_op jit(solution)/shard_map/ppermute | solution.py:10
  491.8 4.5 copy-start.3
  496.3 219.7 %collective-permute-start.3 = (f32[2,512,1024]{2,1,0:T(8,128)}, f32[2,512,1024]{2,1,0:T(8,128)}, u32[]{:S(2)}, u32[]{:S(2)}) collective-permute-start(f32[2,512,1024]{2,1,0:T(8,128)} %slice.141), channel_id=1, source_target_pairs={{0,8},{8,16},{16,24},{24,32},{32,40},{40,48},{48,56},{56,64},{64,7... | collective-permute-start | bytes 12582920 | tf_op jit(solution)/shard_map/ppermute | solution.py:10
Sparse Core Ops, SparseCore 0:
  496.5 216.3 all-reduce.1
where the time goes:
time: 733 us; the launch traced here: 730 us
  waiting for transfers between devices  379 us (52%)
  local copies, waits for them, and re-layouts  129 us (18%)
  other arithmetic  109 us (15%)
  matrix products  66.5 us (9%)
  loops' own time  23.5 us (3%)
  between operations  14.1 us (2%)
  starting transfers between devices  8.45 us (1%)
    psum x1, waiting for transfers between devices, body(): summed = lax.psum(probe_sum, ('scan', 'tile'))  217 us
    ppermute x4, waiting for transfers between devices, shifted(): return lax.ppermute(value, axis, pairs)  163 us
    dynamic_update_slice x6, local copies, waits for them, and re-layouts, visit(): lax.dynamic_update_slice(gradient, current + update, (anchor, row_start,...  86.1 us
    dot_general x12, matrix products, right_product(): jnp.einsum('dub,dcbv->cuv', planes, table, preferred_element_type=jnp.flo...  66.5 us
    another operation x1, loops' own time, body(): gradient, probe_sum = lax.fori_loop(0, count, visit, start)  23.5 us
    another operation x6, other arithmetic  22.6 us
    add x6, other arithmetic, visit(): patch[0] * wave[0] + patch[1] * wave[1]  21.6 us
    add x6, other arithmetic, visit(): current + update  18.5 us
  transfers between devices with their start and end apart: 5, of which 4 were waited for; matrix products, arithmetic and copies ran while one was open for 3% of the time, Pallas kernels for 0%

commit v1 on v0

v1 whole, which is shorter than its diff:
```python
import jax
import jax.numpy as jnp
import ml_dtypes
import numpy as np
from jax import lax
from jax.sharding import PartitionSpec as P
from jax.experimental import pallas as pl
from jax.experimental.pallas import tpu as pltpu

M = 512
Q4 = 128


def kernel_tables():
    counter = np.arange(M, dtype=np.int64)
    product = counter[:, None] * counter[None, :] % M
    angles = product.astype(np.float32) * np.float32(2.0 * 3.141592653589793 / M)
    norm_scale = np.float32(1.0) / np.sqrt(np.float32(M))
    cosine, sine = np.cos(angles) * norm_scale, np.sin(angles) * norm_scale
    classes = range(4)
    first = np.concatenate([np.arange(m, Q4, 4) for m in classes])
    c, s = cosine[first], sine[first]
    left1 = np.stack([np.block([[c[:, m::4], s[:, m::4]], [-s[:, m::4], c[:, m::4]]]) for m in classes])
    order = np.concatenate([np.arange(m, M, 4) for m in classes])
    c, s = cosine[:, order], sine[:, order]
    right2 = np.block([[c, -s], [s, c]])
    c, s = cosine[:Q4], sine[:Q4]
    left3 = np.stack([np.block([[c[:, m::4], -s[:, m::4]], [s[:, m::4], c[:, m::4]]]) for m in classes])
    c, s = cosine[:, :Q4], sine[:, :Q4]
    right4 = np.stack([np.block([[c[m::4], s[m::4]], [-s[m::4], c[m::4]]]) for m in classes])
    return [jnp.asarray(t.astype(ml_dtypes.bfloat16)) for t in (left1, right2, left3, right4)]


def mm(a, b):
    return jnp.dot(a, b, preferred_element_type=jnp.float32)


def butterfly(e, sign):
    (r0, i0), (r1, i1), (r2, i2), (r3, i3) = e
    ar, ai, br, bi = r0 + r2, i0 + i2, r0 - r2, i0 - i2
    cr, ci, dr, di = r1 + r3, i1 + i3, r1 - r3, i1 - i3
    plus = (br - di, bi + dr)
    minus = (br + di, bi - dr)
    one, three = (plus, minus) if sign > 0 else (minus, plus)
    return [(ar + cr, ai + ci), one, (ar - cr, ai - ci), three]


def spans(pieces, vmem):
    for ref, row, col in pieces:
        for b in range(ref.shape[2] // 128):
            there = vmem.at[:, col // 128 + b, row:row + ref.shape[1], :]
            yield ref.at[:, :, 128 * b:128 * (b + 1)], there


def kernel(row_ref, col_ref, own, low_left, far_left, low_right, far_right, beside, corner_near, corner_far,
           probe, probe4, amp, left1, right2, left3, right4,
           g_own, g_left, g_right, g_beside, g_corner, psum,
           ext, grad, zs, ps, es, hs, qs, xs, gs, sems):
    step = pl.program_id(0)
    last = pl.num_programs(0) - 1
    rows = own.shape[1]
    cols = own.shape[2]
    wide = ext.shape[1]
    near = rows + low_left.shape[1]
    inputs = (
        (own, 0, 0), (low_left, rows, 0), (far_left, near, 0), (low_right, rows, M), (far_right, near, M),
        (beside, 0, cols), (corner_near, rows, cols), (corner_far, near, cols),
    )
    outputs = ((g_own, 0, 0), (g_left, rows, 0), (g_right, rows, M), (g_beside, 0, cols), (g_corner, rows, cols))

    @pl.when(step == 0)
    def _():
        for n, (src, dst) in enumerate(spans(inputs, ext)):
            pltpu.make_async_copy(src, dst, sems.at[n]).start()

        def clear(i, _):
            base = pl.multiple_of(i * 8, 8)
            for p in range(2):
                for b in range(wide):
                    grad[p, b, pl.ds(base, 8), :] = jnp.zeros((8, 128), jnp.float32)
            return 0
        lax.fori_loop(0, grad.shape[2] // 8, clear, 0)

        def clear2(i, _):
            base = pl.multiple_of(i * 8, 8)
            for p in range(2):
                psum[p, pl.ds(base, 8), :] = jnp.zeros((8, M), jnp.float32)
            return 0
        lax.fori_loop(0, M // 8, clear2, 0)
        for n, (src, dst) in enumerate(spans(inputs, ext)):
            pltpu.make_async_copy(src, dst, sems.at[n]).wait()

    r = row_ref[step]
    c = col_ref[step]
    cb = c // 128
    dc = c - cb * 128
    R = 128

    def take(i, _):
        base = pl.multiple_of(i * R, R)
        lane = lax.broadcasted_iota(jnp.int32, (R, 128), 1)
        keep = lane < 128 - dc
        for p in range(2):
            parts = [
                pltpu.roll(ext[p, cb + b, pl.ds(r + base, R), :], 128 - dc, 1)
                for b in range(5)
            ]
            for b in range(4):
                zs[p, b, pl.ds(base, R), :] = jnp.where(keep, parts[b], parts[b + 1])
        return 0
    lax.fori_loop(0, M // R, take, 0)

    def psi(i, _):
        base = pl.multiple_of(i * 16, 16)
        for m in range(4):
            for b in range(4):
                at = slice(128 * b, 128 * (b + 1))
                zr = zs[0, b, pl.ds(base * 4 + m, 16, stride=4), :]
                zi = zs[1, b, pl.ds(base * 4 + m, 16, stride=4), :]
                pr = probe4[0, m, pl.ds(base, 16), at]
                pi = probe4[1, m, pl.ds(base, 16), at]
                ps[m, pl.ds(base, 16), at] = (pr * zr - pi * zi).astype(jnp.bfloat16)
                ps[m, pl.ds(base + Q4, 16), at] = (pr * zi + pi * zr).astype(jnp.bfloat16)
        return 0
    lax.fori_loop(0, Q4 // 16, psi, 0)

    for m in range(4):
        es[m] = mm(left1[m], ps[m])

    def half(i, _):
        base = pl.multiple_of(i * 16, 16)
        e = [(es[m, pl.ds(base, 16), :], es[m, pl.ds(base + Q4, 16), :]) for m in range(4)]
        for j, (re, im) in enumerate(butterfly(e, -1)):
            hs[pl.ds(base + Q4 * j, 16), 0:M] = re.astype(jnp.bfloat16)
            hs[pl.ds(base + Q4 * j, 16), M:] = im.astype(jnp.bfloat16)
        return 0
    lax.fori_loop(0, Q4 // 16, half, 0)

    qs[...] = mm(hs[...], right2[...])

    def chi(i, _):
        base = pl.multiple_of(i * 32, 32)
        j, m = i // 4, i % 4
        fr = qs[pl.ds(base, 32), 0:M]
        fi = qs[pl.ds(base, 32), M:]
        inverse = lax.rsqrt(fr * fr + fi * fi)
        factor = 1.0 - amp[0, pl.ds(base, 32), :] * jnp.minimum(inverse, 2.0)
        to = pl.multiple_of(j * 32, 32)
        xs[m, pl.ds(to, 32), :] = (fr * factor).astype(jnp.bfloat16)
        xs[m, pl.ds(to + Q4, 32), :] = (fi * factor).astype(jnp.bfloat16)
        return 0
    lax.fori_loop(0, M // 32, chi, 0)

    for m in range(4):
        es[m] = mm(left3[m], xs[m])

    def back(i, _):
        base = pl.multiple_of(i * 16, 16)
        e = [(es[m, pl.ds(base, 16), :], es[m, pl.ds(base + Q4, 16), :]) for m in range(4)]
        for j, (re, im) in enumerate(butterfly(e, 1)):
            re = re.astype(jnp.bfloat16)
            im = im.astype(jnp.bfloat16)
            for m in range(4):
                gs[m, pl.ds(base + Q4 * j, 16), 0:Q4] = re[:, Q4 * m:Q4 * (m + 1)]
                gs[m, pl.ds(base + Q4 * j, 16), Q4:] = im[:, Q4 * m:Q4 * (m + 1)]
        return 0
    lax.fori_loop(0, Q4 // 16, back, 0)

    for m in range(4):
        qs[:, 256 * m:256 * (m + 1)] = mm(gs[m], right4[m])

    def finish(i, _):
        N = 16
        base = pl.multiple_of(i * N, N)
        at = pl.ds(base, N)
        lane = lax.broadcasted_iota(jnp.int32, (N, 128), 1)
        keep = lane >= dc
        e = [(qs[at, 256 * m:256 * m + Q4], qs[at, 256 * m + Q4:256 * (m + 1)]) for m in range(4)]
        old = [[grad[p, cb + b, pl.ds(r + base, N), :] for b in range(5)] for p in range(2)]
        sums = [[psum[p, at, Q4 * j:Q4 * (j + 1)] for j in range(4)] for p in range(2)]
        rolled = ([], [])
        for j, (wr, wi) in enumerate(butterfly(e, 1)):
            pr = probe[0, at, Q4 * j:Q4 * (j + 1)]
            pi = probe[1, at, Q4 * j:Q4 * (j + 1)]
            zr = zs[0, j, at, :]
            zi = zs[1, j, at, :]
            sums[0][j] += zr * wr + zi * wi
            sums[1][j] += zr * wi - zi * wr
            rolled[0].append(pltpu.roll(pr * wr + pi * wi, dc, 1))
            rolled[1].append(pltpu.roll(pr * wi - pi * wr, dc, 1))
        zero = jnp.zeros((N, 128), jnp.float32)
        for p in range(2):
            u = [zero] + rolled[p] + [zero]
            for b in range(5):
                grad[p, cb + b, pl.ds(r + base, N), :] = old[p][b] + jnp.where(keep, u[b + 1], u[b])
            for j in range(4):
                psum[p, at, Q4 * j:Q4 * (j + 1)] = sums[p][j]
        return 0
    lax.fori_loop(0, M // 16, finish, 0, unroll=4)

    @pl.when(step == last)
    def _():
        for n, (dst, src) in enumerate(spans(outputs, grad)):
            pltpu.make_async_copy(src, dst, sems.at[n]).start()
        for n, (dst, src) in enumerate(spans(outputs, grad)):
            pltpu.make_async_copy(src, dst, sems.at[n]).wait()


def positions(off_rows, off_cols, objects, probe, amps, tables):
    count = amps.shape[0]
    rows, cols = objects[0].shape[1:]
    f32, bf16 = jnp.float32, jnp.bfloat16
    anyspec = pl.BlockSpec(memory_space=pl.ANY)
    whole = lambda shape: pl.BlockSpec(shape, lambda i, *_: (0,) * len(shape))
    probe4 = probe.reshape(2, Q4, 4, M).transpose(0, 2, 1, 3)
    return pl.pallas_call(
        kernel,
        grid_spec=pltpu.PrefetchScalarGridSpec(
            num_scalar_prefetch=2,
            grid=(count,),
            in_specs=[
                *[anyspec] * len(objects),
                whole((2, M, M)), whole((2, 4, Q4, M)),
                pl.BlockSpec((1, M, M), lambda i, *_: (i, 0, 0)),
                whole((4, 256, 256)), whole((1024, 1024)), whole((4, 256, 256)), whole((4, 256, 256)),
            ],
            out_specs=[*[anyspec] * 5, whole((2, M, M))],
            scratch_shapes=[
                pltpu.VMEM((2, (cols + M) // 128, rows + M, 128), f32),
                pltpu.VMEM((2, (cols + M) // 128, rows + M, 128), f32),
                pltpu.VMEM((2, 4, M, 128), f32),
                pltpu.VMEM((4, 256, M), bf16),
                pltpu.VMEM((4, 256, M), f32),
                pltpu.VMEM((M, 2 * M), bf16),
                pltpu.VMEM((M, 2 * M), f32),
                pltpu.VMEM((4, 256, M), bf16),
                pltpu.VMEM((4, M, 256), bf16),
                pltpu.SemaphoreType.DMA((64,)),
            ],
        ),
        out_shape=[
            jax.ShapeDtypeStruct((2, rows, cols), f32),
            *[jax.ShapeDtypeStruct((2, M, M), f32)] * 5,
        ],
        compiler_params=pltpu.CompilerParams(vmem_limit_bytes=60 * 2**20),
        cost_estimate=pl.CostEstimate(flops=6 * 10**9, bytes_accessed=50 * 2**20, transcendentals=0),
        name="positions",
    )(off_rows, off_cols, *objects, probe, probe4, amps, *tables)


def order_kernel(a0, a1, a2, a3, out):
    def body(i, _):
        base = pl.multiple_of(i * 32, 32)
        lane = lax.broadcasted_iota(jnp.int32, (32, 128), 1)
        j, m = i // 4, i % 4
        parts = [a[0, pl.ds(128 * j + m, 32, stride=4), :] for a in (a0, a1, a2, a3)]
        for k in range(4):
            idx = (lane * 4 + k) % 128
            acc = jnp.take_along_axis(parts[0], idx, axis=1)
            for b in range(1, 4):
                acc = jnp.where(lane >= 32 * b, jnp.take_along_axis(parts[b], idx, axis=1), acc)
            out[0, pl.ds(base, 32), 128 * k:128 * (k + 1)] = acc
        return 0
    lax.fori_loop(0, M // 32, body, 0)


def ordered(amps):
    spec = pl.BlockSpec((1, M, M), lambda i: (i, 0, 0))
    part = lambda b: pl.BlockSpec((1, M, 128), lambda i: (i, 0, b))
    return pl.pallas_call(
        order_kernel, grid=(amps.shape[0],), in_specs=[part(b) for b in range(4)], out_specs=spec,
        out_shape=jax.ShapeDtypeStruct(amps.shape, jnp.float32), name="ordered",
        cost_estimate=pl.CostEstimate(flops=10**6, bytes_accessed=12 * 2**20, transcendentals=0),
    )(amps, amps, amps, amps)


def scan_pairs(step, middle=None):
    pairs = []
    for s in range(16):
        z, x = s // 4, s % 4
        z = (z - step) % 4 if x == middle else z
        pairs.append((s, 4 * z + (x + step) % 4))
    return pairs


def rows_below(value):
    return lax.ppermute(value, "scan", [(s, (s - 1) % 16) for s in range(16)])


def rows_above(value):
    return lax.ppermute(value, "scan", [(s, (s + 1) % 16) for s in range(16)])


def detour(value, step):
    stages = []
    for middle in (None, 1 if step > 0 else 2, None):
        value = lax.ppermute(value, "scan", scan_pairs(step, middle))
        stages.append(value)
    return stages


def after(value, *done):
    return lax.optimization_barrier((value, *done))[0]


def tile_shift(value, step):
    return lax.ppermute(value, "tile", [(t, (t + step) % 8) for t in range(8)])


def part(kind):
    s = lax.axis_index("scan")
    t = lax.axis_index("tile")
    return {"core": t % 2, "y": t // 2, "x": s % 4, "z": s // 4}[kind]


def part_pairs(kind, d):
    if kind == "core":
        return "tile", [(t, t ^ 1) for t in range(8)]
    if kind == "y":
        return "tile", [(t, (t // 2 + d) % 4 * 2 + t % 2) for t in range(8)]
    if kind == "x":
        return "scan", [(s, s // 4 * 4 + (s % 4 + d) % 4) for s in range(16)]
    return "scan", [(s, (s // 4 + d) % 4 * 4 + s % 4) for s in range(16)]


def scatter_sum(value, kind):
    n = 2 if kind == "core" else 4
    me = part(kind)
    size = value.shape[0] // n
    total = lax.dynamic_slice_in_dim(value, me * size, size, 0)
    for d in range(1, n):
        piece = lax.dynamic_slice_in_dim(value, (me + d) % n * size, size, 0)
        total = total + lax.ppermute(piece, *part_pairs(kind, d))
    return total


def exchange_sum(value, kind):
    total = value
    for d in range(1, 4):
        total = total + lax.ppermute(value, *part_pairs(kind, d))
    return total


def gather_parts(value, kind):
    n = 2 if kind == "core" else 4
    me = part(kind)
    size = value.shape[0]
    whole = jnp.zeros((n * size,) + value.shape[1:], value.dtype)
    whole = lax.dynamic_update_slice_in_dim(whole, value, me * size, 0)
    for d in range(1, n):
        piece = lax.ppermute(value, *part_pairs(kind, d))
        whole = lax.dynamic_update_slice_in_dim(whole, piece, (me - d) % n * size, 0)
    return whole


def body(object_planes, probe_planes, amplitudes, off_rows, off_cols):
    rows_here = object_planes.shape[1]
    cols_here = object_planes.shape[2]
    count = amplitudes.shape[0]
    near = rows_here * 3 // 4
    left = object_planes[:, :, :M]
    low_left = rows_below(left[:, :near])
    far_left = detour(left[:, near:], 1)[-1]
    low_right = rows_below(object_planes[:, :near, M:])
    far_right = detour(object_planes[:, near:, M:], 1)[-1]
    beside = tile_shift(left, -1)
    amps = ordered(amplitudes)
    low_left, amps = lax.optimization_barrier((low_left, amps))
    corner_near = tile_shift(low_left, -1)
    corner_far = tile_shift(far_left, -1)
    own, lower_left, lower_right, strip, corner, probe_sum = positions(
        off_rows, off_cols,
        (object_planes, low_left, far_left, low_right, far_right, beside, corner_near, corner_far),
        probe_planes, amps, kernel_tables())
    right_near = rows_above(lower_right[:, :near])
    right_hops = detour(lower_right[:, near:], -1)
    corner = tile_shift(corner, 1)
    summed = scatter_sum(probe_sum.reshape(2 * M, M), "core")
    summed = scatter_sum(after(summed, right_hops[0]), "y")
    strip = tile_shift(after(strip, summed), 1)
    summed = exchange_sum(after(summed, right_hops[1], corner), "z")
    summed = exchange_sum(after(summed, right_hops[2], right_near), "x")
    npos_total = count * lax.axis_size("scan") * lax.axis_size("tile")
    summed = summed / jnp.sqrt(jnp.float32(npos_total))
    lower_left = after(lower_left + corner, summed)
    left_near = rows_above(lower_left[:, :near])
    left_hops = detour(lower_left[:, near:], -1)
    summed = gather_parts(summed, "y")
    summed = gather_parts(after(summed, left_hops[0]), "core")
    right_far, left_far = right_hops[2], left_hops[2]
    arrived = jnp.concatenate([
        jnp.concatenate([left_near, left_far], axis=1) + strip,
        jnp.concatenate([right_near, right_far], axis=1),
    ], axis=2)
    return (own + arrived, summed.reshape(2, M, M))


def solution(mesh):
    in_specs = (
        P(None, "scan", "tile"),
        P(),
        P(("scan", "tile"), None, None),
        P(("scan", "tile")),
        P(("scan", "tile")),
    )
    out_specs = (P(None, "scan", "tile"), P())
    return jax.shard_map(body, mesh=mesh, in_specs=in_specs, out_specs=out_specs, check_vma=False)
```

time: 733 us -> 262 us (0.36)
  waiting for transfers between devices: 379 us -> 105 us
  local copies, waits for them, and re-layouts: 129 us -> 19.3 us
  other arithmetic: 109 us -> 12.4 us
  Pallas kernels: 0 us -> 70.2 us
  matrix products: 66.5 us -> 0 us
  starting transfers between devices: 8.45 us -> 52.4 us
  loops' own time: 23.5 us -> 0 us
  between operations: 14.1 us -> 0.96 us
    psum x1 -> x0, waiting for transfers between devices: 217 us -> none  [body(): summed = lax.psum(probe_sum, ('scan', 'tile'))]
    dynamic_update_slice x6 -> x5, local copies, waits for them, and re-layouts: 86.1 us -> 3.34 us  [the longest x4 3.26 us: gather_parts(): lax.dynamic_update_slice_in_dim(whole, piece, (me - d) % n * size, 0)]
    pallas_call x0 -> x2, Pallas kernels: none -> 70.2 us  [the longest x1 52.5 us: positions(): pl.pallas_call(kernel, grid_spec=pltpu.PrefetchScalarGridSpec(num_scalar_...]
    dot_general x12 -> x0, matrix products: 66.5 us -> none  [right_product(): jnp.einsum('dub,dcbv->cuv', planes, table, preferred_element_type=jnp.flo...]
    ppermute x4 -> x35, waiting for transfers between devices: 163 us -> 105 us  [the longest x12 57.8 us: detour(): value = lax.ppermute(value, 'scan', scan_pairs(step, middle))]
    ppermute x4 -> x35, starting transfers between devices: 8.42 us -> 52.4 us  [the longest x5 10.4 us: tile_shift(): return lax.ppermute(value, 'tile', [(t, (t + step) % 8) for t in range(8)])]
    add x13 -> x6, other arithmetic: 46.9 us -> 11.6 us  [the longest x1 4.36 us: body(): return (own + arrived, summed.reshape(2, M, M))]
    another operation x9 -> x0, other arithmetic: 24.6 us -> none
  transfers between devices with their start and end apart: 5 -> 35, of which waited for: 4 -> 19; matrix products, arithmetic and copies ran while one was open for 3% -> 9% of each run, Pallas kernels for 0% -> 7%
where the time goes in v1:
time: 262 us; the launch traced here: 260 us
  waiting for transfers between devices  105 us (40%)
  Pallas kernels  70.2 us (27%)
  starting transfers between devices  52.4 us (20%)
  local copies, waits for them, and re-layouts  19.3 us (7%)
  other arithmetic  12.4 us (5%)
    ppermute x12, waiting for transfers between devices, detour(): value = lax.ppermute(value, 'scan', scan_pairs(step, middle))  57.8 us
    pallas_call x1, Pallas kernels, positions(): pl.pallas_call(kernel, grid_spec=pltpu.PrefetchScalarGridSpec(num_scalar_...  52.5 us
    ppermute x6, waiting for transfers between devices, exchange_sum(): total = total + lax.ppermute(value, *part_pairs(kind, d))  22.6 us
    pallas_call x1, Pallas kernels, ordered(): pl.pallas_call(order_kernel, grid=(amps.shape[0],), in_specs=[part(b) for...  17.6 us
    ppermute x5, starting transfers between devices, tile_shift(): return lax.ppermute(value, 'tile', [(t, (t + step) % 8) for t in range(8)])  10.4 us
    ppermute x2, waiting for transfers between devices, rows_below(): return lax.ppermute(value, 'scan', [(s, (s - 1) % 16) for s in range(16)])  10.3 us
    ppermute x2, starting transfers between devices, rows_below(): return lax.ppermute(value, 'scan', [(s, (s - 1) % 16) for s in range(16)])  9.56 us
    ppermute x4, starting transfers between devices, gather_parts(): piece = lax.ppermute(value, *part_pairs(kind, d))  9.51 us
  transfers between devices with their start and end apart: 35, of which 19 were waited for; matrix products, arithmetic and copies ran while one was open for 9% of the time, Pallas kernels for 7%

profile of v1, /device:TPU:1, one launch (start us, length us, event | category | flops | bytes accessed | tf_op | source)
XLA Modules:
  0.0 260.1 jit_solution(12588892515419222272)
XLA Ops:
  0.6 4.1 %fusion.1 = (f32[2,384,512]{2,1,0:T(8,128)}, f32[2,384,512]{2,1,0:T(8,128)}) fusion(f32[2,512,1024]{2,1,0:T(8,128)} %own.1), kind=kLoop, calls=%fused_computation.18 | loop fusion | bytes 6291456 | tf_op jit(solution)/shard_map/slice | solution.py:364
  4.7 6.8 %collective-permute-start = (f32[2,384,512]{2,1,0:T(8,128)}, f32[2,384,512]{2,1,0:T(8,128)}, u32[]{:S(2)}, u32[]{:S(2)}) collective-permute-start(f32[2,384,512]{2,1,0:T(8,128)} %get-tuple-element.35), channel_id=1, source_target_pairs={{0,120},{8,0},{16,8},{24,16},{32,24},{40,32},{48,40},{56,48},{64,5... | collective-permute-start | bytes 4718600 | tf_op jit(solution)/shard_map/ppermute | solution.py:287
  14.1 2.8 %collective-permute-start.4 = (f32[2,384,512]{2,1,0:T(8,128)}, f32[2,384,512]{2,1,0:T(8,128)}, u32[]{:S(2)}, u32[]{:S(2)}) collective-permute-start(f32[2,384,512]{2,1,0:T(8,128)} %get-tuple-element.34), channel_id=1, source_target_pairs={{0,120},{8,0},{16,8},{24,16},{32,24},{40,32},{48,40},{56,48},{64,5... | collective-permute-start | bytes 4718600 | tf_op jit(solution)/shard_map/ppermute | solution.py:287
  16.9 17.6 %ordered.1.amp = f32[6,512,512]{2,1,0:T(8,128)} custom-call(f32[6,512,512]{2,1,0:T(8,128)} %a3.1, f32[6,512,512]{2,1,0:T(8,128)} %a3.1, f32[6,512,512]{2,1,0:T(8,128)} %a3.1, f32[6,512,512]{2,1,0:T(8,128)} %a3.1), custom_call_target="tpu_custom_call" | custom-call | flops 1000000 | bytes 12582912 | tf_op jit(solution)/shard_map/ordered/pallas_call | solution.py:270
  34.6 10.3 %collective-permute-done.low_left = f32[2,384,512]{2,1,0:T(8,128)} collective-permute-done((f32[2,384,512]{2,1,0:T(8,128)}, f32[2,384,512]{2,1,0:T(8,128)}, u32[]{:S(2)}, u32[]{:S(2)}) %collective-permute-start) | collective-permute-done | bytes 1572896 | tf_op jit(solution)/shard_map/ppermute | solution.py:287
  44.9 2.7 %collective-permute-start.9 = (f32[2,384,512]{2,1,0:T(8,128)}, f32[2,384,512]{2,1,0:T(8,128)}, u32[]{:S(2)}, u32[]{:S(2)}) collective-permute-start(f32[2,384,512]{2,1,0:T(8,128)} %collective-permute-done.low_left), channel_id=1, source_target_pairs={{0,7},{1,0},{2,1},{3,2},{4,3},{5,4},{6,5},{7,6},{8,15},{9,8},{10,9... | collective-permute-start | bytes 4718600 | tf_op jit(solution)/shard_map/ppermute | solution.py:307
  47.6 2.1 collective-permute-start.3
  49.7 12.4 %collective-permute-done.6 = f32[2,128,512]{2,1,0:T(8,128)} collective-permute-done((f32[2,128,512]{2,1,0:T(8,128)}, f32[2,128,512]{2,1,0:T(8,128)}, u32[]{:S(2)}, u32[]{:S(2)}) %collective-permute-start.6) | collective-permute-done | bytes 524320 | tf_op jit(solution)/shard_map/ppermute | solution.py:297
  62.2 11.1 %collective-permute-done.3.far_left = f32[2,128,512]{2,1,0:T(8,128)S(1)} collective-permute-done((f32[2,128,512]{2,1,0:T(8,128)S(1)}, f32[2,128,512]{2,1,0:T(8,128)S(1)}, u32[]{:S(2)}, u32[]{:S(2)}) %collective-permute-start.3) | collective-permute-done | bytes 524320 | tf_op jit(solution)/shard_map/ppermute | solution.py:297
  73.3 2.2 collective-permute-start.10
  77.1 2.6 copy.14
  79.7 4.9 %collective-permute-done.7.far_right = f32[2,128,512]{2,1,0:T(8,128)S(1)} collective-permute-done((f32[2,128,512]{2,1,0:T(8,128)}, f32[2,128,512]{2,1,0:T(8,128)S(1)}, u32[]{:S(2)}, u32[]{:S(2)}) %collective-permute-start.7) | collective-permute-done | bytes 524320 | tf_op jit(solution)/shard_map/ppermute | solution.py:297
  85.4 52.5 %positions.1 = (f32[2,512,1024]{2,1,0:T(8,128)}, f32[2,512,512]{2,1,0:T(8,128)}, f32[2,512,512]{2,1,0:T(8,128)}, f32[2,512,512]{2,1,0:T(8,128)}, f32[2,512,512]{2,1,0:T(8,128)}, /*index=5*/f32[2,512,512]{2,1,0:T(8,128)}) custom-call(s32[6]{0:T(128)} %row_ref.1, s32[6]{0:T(128)} %col_ref.1, f32[2,512,1024]{2,1,0:T(8,128)} %own.1, ...), custom_call_target="tpu_custom_call" | custom-call | flops 6000000000 | bytes 52428800 | tf_op jit(solution)/shard_map/positions/pallas_call | solution.py:216
  137.9 2.5 collective-permute-start.11
  144.7 10.4 %collective-permute-done.13 = f32[2,128,512]{2,1,0:T(8,128)} collective-permute-done((f32[2,128,512]{2,1,0:T(8,128)S(1)}, f32[2,128,512]{2,1,0:T(8,128)}, u32[]{:S(2)}, u32[]{:S(2)}) %collective-permute-start.13) | collective-permute-done | bytes 524320 | tf_op jit(solution)/shard_map/ppermute | solution.py:297
  162.0 5.5 %collective-permute-done.17 = f32[2,128,512]{2,1,0:T(8,128)} collective-permute-done((f32[2,128,512]{2,1,0:T(8,128)}, f32[2,128,512]{2,1,0:T(8,128)}, u32[]{:S(2)}, u32[]{:S(2)}) %collective-permute-start.17) | collective-permute-done | bytes 524320 | tf_op jit(solution)/shard_map/ppermute | solution.py:297
  168.7 3.1 %collective-permute-start.21 = (f32[2,128,512]{2,1,0:T(8,128)}, f32[2,128,512]{2,1,0:T(8,128)S(1)}, u32[]{:S(2)}, u32[]{:S(2)}) collective-permute-start(f32[2,128,512]{2,1,0:T(8,128)} %collective-permute-done.17), channel_id=1, source_target_pairs={{0,24},{8,0},{16,8},{24,16},{32,56},{40,32},{48,40},{56,48},{64,88... | collective-permute-start | bytes 1572872 | tf_op jit(solution)/shard_map/ppermute | solution.py:297
  172.5 4.2 %collective-permute-done.14 = f32[128,512]{1,0:T(8,128)} collective-permute-done((f32[128,512]{1,0:T(8,128)S(1)}, f32[128,512]{1,0:T(8,128)}, u32[]{:S(2)}, u32[]{:S(2)}) %collective-permute-start.14) | collective-permute-done | bytes 262176 | tf_op jit(solution)/shard_map/ppermute | solution.py:333
  177.9 2.7 %collective-permute-start.20 = (f32[128,512]{1,0:T(8,128)S(1)}, f32[128,512]{1,0:T(8,128)S(1)}, u32[]{:S(2)}, u32[]{:S(2)}) collective-permute-start(f32[128,512]{1,0:T(8,128)S(1)} %add_add_fusion.1), channel_id=1, source_target_pairs={{0,96},{8,104},{16,112},{24,120},{32,0},{40,8},{48,16},{56,24},{64... | collective-permute-start | bytes 786440 | tf_op jit(solution)/shard_map/ppermute | solution.py:340
  181.3 4.2 %collective-permute-done.20 = f32[128,512]{1,0:T(8,128)S(1)} collective-permute-done((f32[128,512]{1,0:T(8,128)S(1)}, f32[128,512]{1,0:T(8,128)S(1)}, u32[]{:S(2)}, u32[]{:S(2)}) %collective-permute-start.20) | collective-permute-done | bytes 262176 | tf_op jit(solution)/shard_map/ppermute | solution.py:340
  185.6 4.6 %collective-permute-done.19 = f32[128,512]{1,0:T(8,128)S(1)} collective-permute-done((f32[128,512]{1,0:T(8,128)S(1)}, f32[128,512]{1,0:T(8,128)S(1)}, u32[]{:S(2)}, u32[]{:S(2)}) %collective-permute-start.19) | collective-permute-done | bytes 262176 | tf_op jit(solution)/shard_map/ppermute | solution.py:340
  190.1 3.8 %collective-permute-done.18 = f32[128,512]{1,0:T(8,128)S(1)} collective-permute-done((f32[128,512]{1,0:T(8,128)S(1)}, f32[128,512]{1,0:T(8,128)S(1)}, u32[]{:S(2)}, u32[]{:S(2)}) %collective-permute-start.18) | collective-permute-done | bytes 262176 | tf_op jit(solution)/shard_map/ppermute | solution.py:340
  194.1 2.8 %collective-permute-start.25 = (f32[128,512]{1,0:T(8,128)S(1)}, f32[128,512]{1,0:T(8,128)S(1)}, u32[]{:S(2)}, u32[]{:S(2)}) collective-permute-start(f32[128,512]{1,0:T(8,128)S(1)} %add_add_fusion), channel_id=1, source_target_pairs={{0,24},{8,0},{16,8},{24,16},{32,56},{40,32},{48,40},{56,48},{64,88... | collective-permute-start | bytes 786440 | tf_op jit(solution)/shard_map/ppermute | solution.py:340
  197.5 2.1 collective-permute-start.30
  199.6 2.1 add.117
  204.4 7.3 %collective-permute-done.23 = f32[128,512]{1,0:T(8,128)S(1)} collective-permute-done((f32[128,512]{1,0:T(8,128)S(1)}, f32[128,512]{1,0:T(8,128)S(1)}, u32[]{:S(2)}, u32[]{:S(2)}) %collective-permute-start.23) | collective-permute-done | bytes 262176 | tf_op jit(solution)/shard_map/ppermute | solution.py:340
  214.3 11.2 %collective-permute-done.27 = f32[2,128,512]{2,1,0:T(8,128)S(1)} collective-permute-done((f32[2,128,512]{2,1,0:T(8,128)S(1)}, f32[2,128,512]{2,1,0:T(8,128)S(1)}, u32[]{:S(2)}, u32[]{:S(2)}) %collective-permute-start.27) | collective-permute-done | bytes 524320 | tf_op jit(solution)/shard_map/ppermute | solution.py:297
  228.0 7.2 %collective-permute-done.31 = f32[128,512]{1,0:T(8,128)} collective-permute-done((f32[128,512]{1,0:T(8,128)}, f32[128,512]{1,0:T(8,128)}, u32[]{:S(2)}, u32[]{:S(2)}) %collective-permute-start.31) | collective-permute-done | bytes 262176 | tf_op jit(solution)/shard_map/ppermute | solution.py:351
  235.1 2.3 collective-permute-done.28
  241.0 7.6 %collective-permute-start.34 = (f32[512,512]{1,0:T(8,128)S(1)}, f32[512,512]{1,0:T(8,128)}, u32[]{:S(2)}, u32[]{:S(2)}) collective-permute-start(f32[512,512]{1,0:T(8,128)S(1)} %constant_dynamic-update-slice_fusion.2), channel_id=1, source_target_pairs={{0,1},{1,0},{2,3},{3,2},{4,5},{5,4},{6,7},{7,6},{8,9},{9,8},{10,11... | collective-permute-start | bytes 3145736 | tf_op jit(solution)/shard_map/ppermute | solution.py:351
  250.6 2.5 maximum_add_fusion.1
  253.1 4.4 %maximum_add_fusion = f32[2,512,1024]{2,1,0:T(8,128)} fusion(f32[2,512,1024]{2,1,0:T(8,128)S(1)} %copy-done.2, f32[2,128,512]{2,1,0:T(8,128)S(1)} %copy-done.8, f32[2,384,512]{2,1,0:T(8,128)} %collective-permute-done.22, f32[2,512,512]{2,1,0:T(8,128)S(1)} %maximum_add_fusion.1), kind=kLoop, calls=%fused_computation | loop fusion | flops 3145728 | bytes 12582912 | tf_op jit(solution)/shard_map/add | solution.py:395
  (87 shorter events, 36.7 us)
Async XLA Ops:
  4.7 40.2 %collective-permute-start = (f32[2,384,512]{2,1,0:T(8,128)}, f32[2,384,512]{2,1,0:T(8,128)}, u32[]{:S(2)}, u32[]{:S(2)}) collective-permute-start(f32[2,384,512]{2,1,0:T(8,128)} %get-tuple-element.35), channel_id=1, source_target_pairs={{0,120},{8,0},{16,8},{24,16},{32,24},{40,32},{48,40},{56,48},{64,5... | collective-permute-start | bytes 4718600 | tf_op jit(solution)/shard_map/ppermute | solution.py:287
  11.6 23.0 %collective-permute-start.1 = (f32[2,128,512]{2,1,0:T(8,128)S(1)}, f32[2,128,512]{2,1,0:T(8,128)}, u32[]{:S(2)}, u32[]{:S(2)}) collective-permute-start(f32[2,128,512]{2,1,0:T(8,128)S(1)} %get-tuple-element.33), channel_id=1, source_target_pairs={{0,8},{8,16},{16,24},{24,0},{32,40},{40,48},{48,56},{56,32},{64,72... | collective-permute-start | bytes 1572872 | tf_op jit(solution)/shard_map/ppermute | solution.py:297
  13.2 71.4 %collective-permute-start.8 = (f32[2,512,512]{2,1,0:T(8,128)}, f32[2,512,512]{2,1,0:T(8,128)}, u32[]{:S(2)}, u32[]{:S(2)}) collective-permute-start(f32[2,512,512]{2,1,0:T(8,128)} %slice.33), channel_id=1, source_target_pairs={{0,7},{1,0},{2,1},{3,2},{4,3},{5,4},{6,5},{7,6},{8,15},{9,8},{10,9... | collective-permute-start | bytes 6291464 | tf_op jit(solution)/shard_map/ppermute | solution.py:307
  14.1 70.4 %collective-permute-start.4 = (f32[2,384,512]{2,1,0:T(8,128)}, f32[2,384,512]{2,1,0:T(8,128)}, u32[]{:S(2)}, u32[]{:S(2)}) collective-permute-start(f32[2,384,512]{2,1,0:T(8,128)} %get-tuple-element.34), channel_id=1, source_target_pairs={{0,120},{8,0},{16,8},{24,16},{32,24},{40,32},{48,40},{56,48},{64,5... | collective-permute-start | bytes 4718600 | tf_op jit(solution)/shard_map/ppermute | solution.py:287
  16.9 30.7 %collective-permute-start.5 = (f32[2,128,512]{2,1,0:T(8,128)S(1)}, f32[2,128,512]{2,1,0:T(8,128)}, u32[]{:S(2)}, u32[]{:S(2)}) collective-permute-start(f32[2,128,512]{2,1,0:T(8,128)S(1)} %get-tuple-element.32), channel_id=1, source_target_pairs={{0,8},{8,16},{16,24},{24,0},{32,40},{40,48},{48,56},{56,32},{64,72... | collective-permute-start | bytes 1572872 | tf_op jit(solution)/shard_map/ppermute | solution.py:297
  34.6 13.0 %collective-permute-start.2 = (f32[2,128,512]{2,1,0:T(8,128)}, f32[2,128,512]{2,1,0:T(8,128)S(1)}, u32[]{:S(2)}, u32[]{:S(2)}) collective-permute-start(f32[2,128,512]{2,1,0:T(8,128)} %collective-permute-done.1), channel_id=1, source_target_pairs={{0,8},{8,112},{16,24},{24,0},{32,40},{40,16},{48,56},{56,32},{64,7... | collective-permute-start | bytes 1572872 | tf_op jit(solution)/shard_map/ppermute | solution.py:297
  44.9 39.7 %collective-permute-start.9 = (f32[2,384,512]{2,1,0:T(8,128)}, f32[2,384,512]{2,1,0:T(8,128)}, u32[]{:S(2)}, u32[]{:S(2)}) collective-permute-start(f32[2,384,512]{2,1,0:T(8,128)} %collective-permute-done.low_left), channel_id=1, source_target_pairs={{0,7},{1,0},{2,1},{3,2},{4,3},{5,4},{6,5},{7,6},{8,15},{9,8},{10,9... | collective-permute-start | bytes 4718600 | tf_op jit(solution)/shard_map/ppermute | solution.py:307
  47.6 14.6 %collective-permute-start.6 = (f32[2,128,512]{2,1,0:T(8,128)}, f32[2,128,512]{2,1,0:T(8,128)}, u32[]{:S(2)}, u32[]{:S(2)}) collective-permute-start(f32[2,128,512]{2,1,0:T(8,128)} %collective-permute-done.5), channel_id=1, source_target_pairs={{0,8},{8,112},{16,24},{24,0},{32,40},{40,16},{48,56},{56,32},{64,7... | collective-permute-start | bytes 1572872 | tf_op jit(solution)/shard_map/ppermute | solution.py:297
  47.6 25.7 %collective-permute-start.3 = (f32[2,128,512]{2,1,0:T(8,128)S(1)}, f32[2,128,512]{2,1,0:T(8,128)S(1)}, u32[]{:S(2)}, u32[]{:S(2)}) collective-permute-start(f32[2,128,512]{2,1,0:T(8,128)S(1)} %collective-permute-done.2), channel_id=1, source_target_pairs={{0,8},{8,16},{16,24},{24,0},{32,40},{40,48},{48,56},{56,32},{64,72... | collective-permute-start | bytes 1572872 | tf_op jit(solution)/shard_map/ppermute | solution.py:297
  62.2 22.4 %collective-permute-start.7 = (f32[2,128,512]{2,1,0:T(8,128)}, f32[2,128,512]{2,1,0:T(8,128)S(1)}, u32[]{:S(2)}, u32[]{:S(2)}) collective-permute-start(f32[2,128,512]{2,1,0:T(8,128)} %collective-permute-done.6), channel_id=1, source_target_pairs={{0,8},{8,16},{16,24},{24,0},{32,40},{40,48},{48,56},{56,32},{64,72... | collective-permute-start | bytes 1572872 | tf_op jit(solution)/shard_map/ppermute | solution.py:297
  73.3 11.2 %collective-permute-start.10 = (f32[2,128,512]{2,1,0:T(8,128)S(1)}, f32[2,128,512]{2,1,0:T(8,128)}, u32[]{:S(2)}, u32[]{:S(2)}) collective-permute-start(f32[2,128,512]{2,1,0:T(8,128)S(1)} %collective-permute-done.3.far_left), channel_id=1, source_target_pairs={{0,7},{1,0},{2,1},{3,2},{4,3},{5,4},{6,5},{7,6},{8,15},{9,8},{10,9... | collective-permute-start | bytes 1572872 | tf_op jit(solution)/shard_map/ppermute | solution.py:307
  137.9 40.0 %collective-permute-start.11 = (f32[2,512,512]{2,1,0:T(8,128)}, f32[2,512,512]{2,1,0:T(8,128)}, u32[]{:S(2)}, u32[]{:S(2)}) collective-permute-start(f32[2,512,512]{2,1,0:T(8,128)} %get-tuple-element.20), channel_id=1, source_target_pairs={{0,1},{1,2},{2,3},{3,4},{4,5},{5,6},{6,7},{7,0},{8,9},{9,10},{10,1... | collective-permute-start | bytes 6291464 | tf_op jit(solution)/shard_map/ppermute | solution.py:307
  141.7 14.9 %collective-permute-start.12 = (f32[512,512]{1,0:T(8,128)S(1)}, f32[512,512]{1,0:T(8,128)}, u32[]{:S(2)}, u32[]{:S(2)}) collective-permute-start(f32[512,512]{1,0:T(8,128)S(1)} %constant_dynamic-slice_fusion.3), channel_id=1, source_target_pairs={{0,1},{1,0},{2,3},{3,2},{4,5},{5,4},{6,7},{7,6},{8,9},{9,8},{10,11... | collective-permute-start | bytes 3145736 | tf_op jit(solution)/shard_map/ppermute | solution.py:333
  141.9 13.2 %collective-permute-start.13 = (f32[2,128,512]{2,1,0:T(8,128)S(1)}, f32[2,128,512]{2,1,0:T(8,128)}, u32[]{:S(2)}, u32[]{:S(2)}) collective-permute-start(f32[2,128,512]{2,1,0:T(8,128)S(1)} %slice.34), channel_id=1, source_target_pairs={{0,24},{8,0},{16,8},{24,16},{32,56},{40,32},{48,40},{56,48},{64,88... | collective-permute-start | bytes 1572872 | tf_op jit(solution)/shard_map/ppermute | solution.py:297
  143.2 50.8 %collective-permute-start.22 = (f32[2,384,512]{2,1,0:T(8,128)}, f32[2,384,512]{2,1,0:T(8,128)}, u32[]{:S(2)}, u32[]{:S(2)}) collective-permute-start(f32[2,384,512]{2,1,0:T(8,128)} %slice.35), channel_id=1, source_target_pairs={{0,8},{8,16},{16,24},{24,32},{32,40},{40,48},{48,56},{56,64},{64,7... | collective-permute-start | bytes 4718600 | tf_op jit(solution)/shard_map/ppermute | solution.py:291
  155.1 12.4 %collective-permute-start.17 = (f32[2,128,512]{2,1,0:T(8,128)}, f32[2,128,512]{2,1,0:T(8,128)}, u32[]{:S(2)}, u32[]{:S(2)}) collective-permute-start(f32[2,128,512]{2,1,0:T(8,128)} %collective-permute-done.13), channel_id=1, source_target_pairs={{0,24},{8,0},{16,40},{24,16},{32,56},{40,32},{48,72},{56,48},{64,8... | collective-permute-start | bytes 1572872 | tf_op jit(solution)/shard_map/ppermute | solution.py:297
  158.9 9.8 %collective-permute-start.16 = (f32[128,512]{1,0:T(8,128)}, f32[128,512]{1,0:T(8,128)}, u32[]{:S(2)}, u32[]{:S(2)}) collective-permute-start(f32[128,512]{1,0:T(8,128)} %get-tuple-element.37), channel_id=1, source_target_pairs={{0,6},{1,7},{2,0},{3,1},{4,2},{5,3},{6,4},{7,5},{8,14},{9,15},{10,... | collective-permute-start | bytes 786440 | tf_op jit(solution)/shard_map/ppermute | solution.py:333
  160.7 11.8 %collective-permute-start.15 = (f32[128,512]{1,0:T(8,128)}, f32[128,512]{1,0:T(8,128)}, u32[]{:S(2)}, u32[]{:S(2)}) collective-permute-start(f32[128,512]{1,0:T(8,128)} %get-tuple-element.38), channel_id=1, source_target_pairs={{0,4},{1,5},{2,6},{3,7},{4,0},{5,1},{6,2},{7,3},{8,12},{9,13},{10,... | collective-permute-start | bytes 786440 | tf_op jit(solution)/shard_map/ppermute | solution.py:333
  167.5 9.3 %collective-permute-start.14 = (f32[128,512]{1,0:T(8,128)S(1)}, f32[128,512]{1,0:T(8,128)}, u32[]{:S(2)}, u32[]{:S(2)}) collective-permute-start(f32[128,512]{1,0:T(8,128)S(1)} %get-tuple-element.36), channel_id=1, source_target_pairs={{0,2},{1,3},{2,4},{3,5},{4,6},{5,7},{6,0},{7,1},{8,10},{9,11},{10,... | collective-permute-start | bytes 786440 | tf_op jit(solution)/shard_map/ppermute | solution.py:333
  168.7 25.3 %collective-permute-start.21 = (f32[2,128,512]{2,1,0:T(8,128)}, f32[2,128,512]{2,1,0:T(8,128)S(1)}, u32[]{:S(2)}, u32[]{:S(2)}) collective-permute-start(f32[2,128,512]{2,1,0:T(8,128)} %collective-permute-done.17), channel_id=1, source_target_pairs={{0,24},{8,0},{16,8},{24,16},{32,56},{40,32},{48,40},{56,48},{64,88... | collective-permute-start | bytes 1572872 | tf_op jit(solution)/shard_map/ppermute | solution.py:297
  180.7 9.5 %collective-permute-start.19 = (f32[128,512]{1,0:T(8,128)S(1)}, f32[128,512]{1,0:T(8,128)S(1)}, u32[]{:S(2)}, u32[]{:S(2)}) collective-permute-start(f32[128,512]{1,0:T(8,128)S(1)} %add_add_fusion.1), channel_id=1, source_target_pairs={{0,64},{8,72},{16,80},{24,88},{32,96},{40,104},{48,112},{56,120},{... | collective-permute-start | bytes 786440 | tf_op jit(solution)/shard_map/ppermute | solution.py:340
  180.7 13.3 %collective-permute-start.18 = (f32[128,512]{1,0:T(8,128)S(1)}, f32[128,512]{1,0:T(8,128)S(1)}, u32[]{:S(2)}, u32[]{:S(2)}) collective-permute-start(f32[128,512]{1,0:T(8,128)S(1)} %add_add_fusion.1), channel_id=1, source_target_pairs={{0,32},{8,40},{16,48},{24,56},{32,64},{40,72},{48,80},{56,88},{64,... | collective-permute-start | bytes 786440 | tf_op jit(solution)/shard_map/ppermute | solution.py:340
  194.1 9.2 %collective-permute-start.25 = (f32[128,512]{1,0:T(8,128)S(1)}, f32[128,512]{1,0:T(8,128)S(1)}, u32[]{:S(2)}, u32[]{:S(2)}) collective-permute-start(f32[128,512]{1,0:T(8,128)S(1)} %add_add_fusion), channel_id=1, source_target_pairs={{0,24},{8,0},{16,8},{24,16},{32,56},{40,32},{48,40},{56,48},{64,88... | collective-permute-start | bytes 786440 | tf_op jit(solution)/shard_map/ppermute | solution.py:340
  196.8 14.8 %collective-permute-start.23 = (f32[128,512]{1,0:T(8,128)S(1)}, f32[128,512]{1,0:T(8,128)S(1)}, u32[]{:S(2)}, u32[]{:S(2)}) collective-permute-start(f32[128,512]{1,0:T(8,128)S(1)} %add_add_fusion), channel_id=1, source_target_pairs={{0,8},{8,16},{16,24},{24,0},{32,40},{40,48},{48,56},{56,32},{64,72... | collective-permute-start | bytes 786440 | tf_op jit(solution)/shard_map/ppermute | solution.py:340
  197.5 51.5 %collective-permute-start.30 = (f32[2,512,512]{2,1,0:T(8,128)}, f32[2,512,512]{2,1,0:T(8,128)}, u32[]{:S(2)}, u32[]{:S(2)}) collective-permute-start(f32[2,512,512]{2,1,0:T(8,128)} %get-tuple-element.28), channel_id=1, source_target_pairs={{0,1},{1,2},{2,3},{3,4},{4,5},{5,6},{6,7},{7,0},{8,9},{9,10},{10,1... | collective-permute-start | bytes 6291464 | tf_op jit(solution)/shard_map/ppermute | solution.py:307
  212.6 12.9 %collective-permute-start.27 = (f32[2,128,512]{2,1,0:T(8,128)S(1)}, f32[2,128,512]{2,1,0:T(8,128)S(1)}, u32[]{:S(2)}, u32[]{:S(2)}) collective-permute-start(f32[2,128,512]{2,1,0:T(8,128)S(1)} %slice.37), channel_id=1, source_target_pairs={{0,24},{8,0},{16,8},{24,16},{32,56},{40,32},{48,40},{56,48},{64,88... | collective-permute-start | bytes 1572872 | tf_op jit(solution)/shard_map/ppermute | solution.py:297
  212.8 37.8 %collective-permute-start.26 = (f32[2,384,512]{2,1,0:T(8,128)S(1)}, f32[2,384,512]{2,1,0:T(8,128)}, u32[]{:S(2)}, u32[]{:S(2)}) collective-permute-start(f32[2,384,512]{2,1,0:T(8,128)S(1)} %slice.36), channel_id=1, source_target_pairs={{0,8},{8,16},{16,24},{24,32},{32,40},{40,48},{48,56},{56,64},{64,7... | collective-permute-start | bytes 4718600 | tf_op jit(solution)/shard_map/ppermute | solution.py:291
  225.5 12.0 %collective-permute-start.28 = (f32[2,128,512]{2,1,0:T(8,128)S(1)}, f32[2,128,512]{2,1,0:T(8,128)}, u32[]{:S(2)}, u32[]{:S(2)}) collective-permute-start(f32[2,128,512]{2,1,0:T(8,128)S(1)} %collective-permute-done.27), channel_id=1, source_target_pairs={{0,24},{8,0},{16,40},{24,16},{32,56},{40,32},{48,72},{56,48},{64,8... | collective-permute-start | bytes 1572872 | tf_op jit(solution)/shard_map/ppermute | solution.py:297
  226.0 9.1 %collective-permute-start.31 = (f32[128,512]{1,0:T(8,128)}, f32[128,512]{1,0:T(8,128)}, u32[]{:S(2)}, u32[]{:S(2)}) collective-permute-start(f32[128,512]{1,0:T(8,128)} %get-tuple-element.31), channel_id=1, source_target_pairs={{0,2},{1,3},{2,4},{3,5},{4,6},{5,7},{6,0},{7,1},{8,10},{9,11},{10,... | collective-permute-start | bytes 786440 | tf_op jit(solution)/shard_map/ppermute | solution.py:351
  226.0 13.5 %collective-permute-start.32 = (f32[128,512]{1,0:T(8,128)}, f32[128,512]{1,0:T(8,128)}, u32[]{:S(2)}, u32[]{:S(2)}) collective-permute-start(f32[128,512]{1,0:T(8,128)} %get-tuple-element.31), channel_id=1, source_target_pairs={{0,4},{1,5},{2,6},{3,7},{4,0},{5,1},{6,2},{7,3},{8,12},{9,13},{10,... | collective-permute-start | bytes 786440 | tf_op jit(solution)/shard_map/ppermute | solution.py:351
  237.5 11.5 %collective-permute-start.29 = (f32[2,128,512]{2,1,0:T(8,128)}, f32[2,128,512]{2,1,0:T(8,128)S(1)}, u32[]{:S(2)}, u32[]{:S(2)}) collective-permute-start(f32[2,128,512]{2,1,0:T(8,128)} %collective-permute-done.28), channel_id=1, source_target_pairs={{0,24},{8,0},{16,8},{24,16},{32,56},{40,32},{48,40},{56,48},{64,88... | collective-permute-start | bytes 1572872 | tf_op jit(solution)/shard_map/ppermute | solution.py:297
  241.0 16.5 %collective-permute-start.34 = (f32[512,512]{1,0:T(8,128)S(1)}, f32[512,512]{1,0:T(8,128)}, u32[]{:S(2)}, u32[]{:S(2)}) collective-permute-start(f32[512,512]{1,0:T(8,128)S(1)} %constant_dynamic-update-slice_fusion.2), channel_id=1, source_target_pairs={{0,1},{1,0},{2,3},{3,2},{4,5},{5,4},{6,7},{7,6},{8,9},{9,8},{10,11... | collective-permute-start | bytes 3145736 | tf_op jit(solution)/shard_map/ppermute | solution.py:351
  (14 other events, 170.5 us)
